TPU v7x, 256 devices: a whole 4x4x8 slice. The times are simulated.
256 devices in a mesh: row: 8 (over z_lo, core), col: 8 (over x, z_hi), fsdp: 4 (over y).
Axes of the slice: x: 4, y: 4, z: 8 (z_hi: 2, z_lo: 4; z = z_hi * 4 + z_lo), core: 2. Of those that a mesh axis runs over, the one named last changes fastest.
Arguments:
- video: bfloat16 [4, 3, 64, 256, 256], P('fsdp', None, 'row', 'col'), may hold values from -6 to 6
- kernel: bfloat16 [6912, 256], P(None, 'fsdp'), may hold values from -0.078125 to 0.078125
- bias_vec: float32 [256], replicated, may hold values from -3 to 3
- cotangent: bfloat16 [4, 3, 32, 128, 256], P('fsdp', None, 'row', 'col'), may hold values from -6 to 6
Outputs:
- activated: bfloat16 [4, 3, 32, 128, 256], P('fsdp', None, 'row', 'col')
- video_grad: bfloat16 [4, 3, 64, 256, 256], P('fsdp', None, 'row', 'col')
- kernel_grad: float32 [6912, 256], P(('row', 'col'), 'fsdp')
- bias_grad: float32 [256], replicated
All inputs are finite; a program needn't handle non-finite values.
Results may differ from a plain program's by a relative error of at most 0.007.
Values may be sent and summed in bfloat16 or wider, within the bound.
A program may use at most 64 MiB of HBM per device.

v0:
```python
import math

import jax
import jax.numpy as jnp
from jax import lax
from jax.experimental import pallas as pl
from jax.experimental.pallas import tpu as pltpu
from jax.sharding import PartitionSpec as P

MESH = pl.DeviceIdType.MESH
F32 = jnp.float32
BF16 = jnp.bfloat16

TAPS = 27
CI = 256
CO = 256
SHARD = 64
KROWS = TAPS * CI
TOK = 192
PITCH = 40
VIA_X = 768
ROUND = 4 * VIA_X
SPAN = (KROWS - ROUND) // 2
BLOCK = 864
WINDOW = 224
PIECE = 108
FACTOR = 1.0 / math.sqrt(49152)


def frame_of(t, p):
    return max(t + p - 2, 0)


def nt(a, b):
    return lax.dot_general(a, b, (((1,), (1,)), ((), ())), preferred_element_type=F32)


def nn(a, b):
    return jnp.dot(a, b, preferred_element_type=F32)


def identity(n):
    rows = lax.broadcasted_iota(jnp.int32, (n, n), 0)
    cols = lax.broadcasted_iota(jnp.int32, (n, n), 1)
    return (rows == cols).astype(F32).astype(BF16)


PLANE = 27 * PITCH


def take(flat, start, count, stride):
    return jnp.concatenate(
        [flat[pl.ds(n * PLANE + start, count, stride=stride), :] for n in range(2)], axis=1
    )


def put(flat, start, count, stride, value):
    for n in range(2):
        flat[pl.ds(n * PLANE + start, count, stride=stride), :] = value[:, 128 * n : 128 * n + 128]


def swap_halves(value):
    return jnp.concatenate(
        [pltpu.roll(value[:, 128 * n : 128 * n + 128], 64, 1) for n in range(value.shape[1] // 128)],
        axis=1,
    )


def kernel_body(
    video,
    kernel,
    bias,
    cot,
    act_out,
    vg_out,
    kg_out,
    bg_out,
    kt,
    vid,
    cotv,
    biasv,
    vpad,
    hl_send,
    hc_send,
    hl,
    hu,
    hc,
    patches,
    pt,
    pts,
    dl,
    dlx,
    dls,
    dlsx,
    w,
    ra,
    rb,
    ya,
    xb,
    ys,
    xs,
    sa,
    sb,
    ra2,
    rb2,
    tt,
    zz,
    rz,
    by,
    bx,
    bz,
    g,
    gl_send,
    gc_send,
    gu,
    gl,
    gc,
    lsem,
    k_s,
    k_r,
    h_s,
    h_r,
    c_s,
    c_r,
    r1_s,
    r1_r,
    r2_s,
    r2_r,
    r3_s,
    r3_r,
    b_s,
    b_r,
):
    row = lax.axis_index("row")
    col = lax.axis_index("col")
    y = lax.axis_index("fsdp")
    core = lax.rem(row, 2)
    zl = row // 2
    x = col // 2
    zh = lax.rem(col, 2)
    z = zh * 4 + zl

    def to_y(n):
        return {"row": row, "col": col, "fsdp": lax.rem(y + n, 4)}

    def to_x(n):
        return {"row": row, "col": lax.rem(x + n, 4) * 2 + zh, "fsdp": y}

    def to_z(n):
        there = lax.rem(z + n, 8)
        return {
            "row": lax.rem(there, 4) * 2 + core,
            "col": x * 2 + there // 4,
            "fsdp": y,
        }

    def to_tile(rows, cols):
        return {"row": lax.rem(row + rows + 8, 8), "col": lax.rem(col + cols + 8, 8), "fsdp": y}

    sibling = {"row": row + 1 - 2 * core, "col": col, "fsdp": y}

    def remote(src, dst, ss, rs, where):
        return pltpu.make_async_remote_copy(
            src_ref=src, dst_ref=dst, send_sem=ss, recv_sem=rs, device_id=where, device_id_type=MESH
        )

    partners = [to_y(n) for n in (1, 2, 3)] + [to_x(n) for n in (1, 2, 3)]
    partners += [to_z(n) for n in range(1, 8)] + [sibling]
    partners += [to_tile(a, b) for a, b in ((0, 1), (0, -1), (1, 0), (-1, 0), (1, 1), (-1, -1))]
    barrier = pltpu.get_barrier_semaphore()
    for partner in partners:
        pl.semaphore_signal(barrier, inc=1, device_id=partner, device_id_type=MESH)

    own_rows = pl.multiple_of(y * SHARD, SHARD)
    load_k = pltpu.make_async_copy(kernel, kt.at[pl.ds(own_rows, SHARD), :], lsem.at[0])
    load_v = pltpu.make_async_copy(video.at[0], vid, lsem.at[1])
    load_c = pltpu.make_async_copy(cot.at[0], cotv, lsem.at[2])
    load_b = pltpu.make_async_copy(bias, biasv, lsem.at[3])
    load_k.start()
    load_v.start()
    load_c.start()
    load_b.start()

    pl.semaphore_wait(barrier, len(partners))

    half_rows = pl.multiple_of(y * SHARD + core * 32, 32)
    via = pl.multiple_of(x * VIA_X, 128)

    def shard_rows(n):
        return pl.multiple_of(lax.rem(y + n, 4) * SHARD + core * 32, 32)

    def other_rows(n):
        return pl.multiple_of(lax.rem(y + n, 4) * SHARD + (1 - core) * 32, 32)

    near = pl.ds(core * 32, 32)
    first = []
    for n in (1, 3, 2):
        first.append(
            remote(
                kernel.at[near, pl.ds(via, VIA_X)],
                kt.at[pl.ds(half_rows, 32), pl.ds(via, VIA_X)],
                k_s.at[n - 1],
                k_r.at[n - 1],
                to_y(n),
            )
        )
        first[-1].start()
    direct = []
    for slot, (n, part) in enumerate(((1, 0), (3, 1), (1, 1), (3, 0))):
        lanes = pl.ds(ROUND + part * SPAN, SPAN)
        direct.append(
            remote(
                kernel.at[near, lanes],
                kt.at[pl.ds(half_rows, 32), lanes],
                k_s.at[3 + slot],
                k_r.at[3 + slot],
                to_y(n),
            )
        )
        direct[-1].start()

    load_v.wait()
    for f in range(3):
        for r in range(8):
            for n in range(2):
                vpad[n, (r + 1) * 3 + f, 8:40, :] = vid[f, r, :, 128 * n : 128 * n + 128].astype(F32)
    flat = vpad.reshape(2 * PLANE, 128)
    hl_send[...] = take(flat, 3 * PITCH + 39, 24, PITCH)
    hc_send[0:3, :] = hl_send[21:24, :]

    halos = [
        remote(hl_send, hl, h_s.at[0], h_r.at[0], to_tile(0, 1)),
        remote(vid.at[:, 7], hu, h_s.at[1], h_r.at[1], to_tile(1, 0)),
        remote(hc_send, hc, h_s.at[2], h_r.at[2], to_tile(1, 1)),
    ]
    for copy in halos:
        copy.start()

    passed = []

    def pass_on(n, start, size, slot):
        ref = kt.at[pl.ds(shard_rows(n), 32), pl.ds(start, size)]
        passed.append(remote(ref, ref, c_s.at[slot], c_r.at[slot], sibling))
        passed[-1].start()

    relayed = []
    for at, n in enumerate((1, 3, 2)):
        first[at].wait_recv()
        ref = kt.at[pl.ds(shard_rows(4 - n), 32), pl.ds(via, VIA_X)]
        for m in (1, 3, 2):
            slot = 9 + (n - 1) * 3 + m - 1
            relayed.append(remote(ref, ref, k_s.at[slot], k_r.at[slot], to_x(m)))
            relayed[-1].start()
        pass_on(4 - n, via, VIA_X, 4 + n)

    forward = []
    for slot, (n, part) in enumerate(((1, 0), (3, 1))):
        direct[slot].wait_recv()
        ref = kt.at[pl.ds(shard_rows(4 - n), 32), pl.ds(ROUND + part * SPAN, SPAN)]
        forward.append(remote(ref, ref, k_s.at[7 + slot], k_r.at[7 + slot], to_y(n)))
        forward[-1].start()
        pass_on(4 - n, ROUND + part * SPAN, SPAN, 17 + slot)

    for copy in halos:
        copy.wait_recv()
    for f in range(3):
        top = hu[f].astype(F32)
        top = jnp.where(row > 0, top, 0.0)
        for n in range(2):
            vpad[n, f, 8:40, :] = top[:, 128 * n : 128 * n + 128]
    put(flat, 3 * PITCH + 7, 24, PITCH, jnp.where(col > 0, hl[...], 0.0))
    corner = jnp.where((row > 0) & (col > 0), hc[...], 0.0)
    for f in range(3):
        for n in range(2):
            vpad[n, f, 7:8, :] = corner[f : f + 1, 128 * n : 128 * n + 128]
    for r in range(9):
        for f in range(3):
            for s in range(3):
                block = take(flat, (r * 3 + f) * PITCH + 7 + s, 16, 2).astype(BF16)
                for t in range(3):
                    for p in range(3):
                        if frame_of(t, p) != f:
                            continue
                        for q in range(3):
                            i, odd = divmod(r - q, 2)
                            if odd or not 0 <= i < 4:
                                continue
                            tap = (p * 3 + q) * 3 + s
                            patches[
                                (t * 4 + i) * 16 : (t * 4 + i) * 16 + 16, tap * CI : tap * CI + CI
                            ] = block
    unit = identity(CI)
    for tap in range(TAPS):
        pt[tap * CI : tap * CI + CI, :] = nt(unit, patches[:, tap * CI : tap * CI + CI]).astype(BF16)
    swaps = []
    for n in range(4):
        base = pl.multiple_of(n * 2 * BLOCK + (1 - core) * BLOCK, 32)
        swaps.append(remote(pt.at[pl.ds(base, BLOCK), :], pts.at[n], c_s.at[n], c_r.at[n], sibling))
        swaps[-1].start()

    def pass_relayed(at, n):
        for k, m in enumerate((1, 3, 2)):
            relayed[at * 3 + k].wait_recv()
            from_x = pl.multiple_of(lax.rem(x + 4 - m, 4) * VIA_X, 128)
            pass_on(4 - n, from_x, VIA_X, 8 + (n - 1) * 3 + m - 1)

    pass_relayed(0, 1)
    pass_relayed(1, 3)
    for slot, (n, part) in ((2, (1, 1)), (3, (3, 0))):
        direct[slot].wait_recv()
        pass_on(4 - n, ROUND + part * SPAN, SPAN, 17 + slot)
    pass_relayed(2, 2)
    for part in range(2):
        forward[part].wait_recv()
        pass_on(2, ROUND + part * SPAN, SPAN, 21 + part)
    for copy in passed:
        copy.wait_recv()
    load_k.wait()

    load_b.wait()
    preact = nt(patches[...], kt[...]) + biasv[...]
    sigma = jax.nn.sigmoid(preact)
    act_out[...] = (preact * sigma).astype(BF16).reshape(1, 3, 4, 16, CO)
    load_c.wait()
    slope = cotv[...].reshape(TOK, CO).astype(F32) * sigma * (1.0 + preact * (1.0 - sigma))
    delta = slope.astype(BF16)
    dl[...] = delta
    swap_delta = remote(dl, dls, c_s.at[4], c_r.at[4], sibling)
    swap_delta.start()
    delta_f = delta.astype(F32)
    dlx[...] = swap_halves(delta_f).astype(BF16)
    bias_own = jnp.sum(delta_f, axis=0, keepdims=True)

    g[...] = jnp.zeros_like(g)
    gflat = g.reshape(2 * PLANE, 128)
    for q in range(3):
        for s in range(3):
            d = [
                nn(dl[...], kt[:, ((p * 3 + q) * 3 + s) * CI : ((p * 3 + q) * 3 + s) * CI + CI])
                for p in range(3)
            ]
            frames = [
                d[0][0:64] + d[0][64:128] + d[0][128:192] + d[1][0:64] + d[1][64:128] + d[2][0:64],
                d[1][128:192] + d[2][64:128],
                d[2][128:192],
            ]
            for f in range(3):
                for i in range(4):
                    at = ((q + 2 * i) * 3 + f) * PITCH + 7 + s
                    sofar = take(gflat, at, 16, 2)
                    put(gflat, at, 16, 2, sofar + frames[f][16 * i : 16 * i + 16])
    gl_send[...] = take(gflat, 3 * PITCH + 7, 24, PITCH)
    for f in range(3):
        for n in range(2):
            gc_send[f : f + 1, 128 * n : 128 * n + 128] = g[n, f, 7:8, :]
    edges = [
        remote(gl_send, gl, h_s.at[3], h_r.at[3], to_tile(0, -1)),
        remote(g.at[:, pl.ds(0, 3), pl.ds(8, 32), :], gu, h_s.at[4], h_r.at[4], to_tile(-1, 0)),
        remote(gc_send, gc, h_s.at[5], h_r.at[5], to_tile(-1, -1)),
    ]
    for copy in edges:
        copy.start()

    swap_delta.wait_recv()
    delta_s = dls[...].astype(F32)
    dlsx[...] = swap_halves(delta_s).astype(BF16)
    bias_chip = bias_own + jnp.sum(delta_s, axis=0, keepdims=True)
    by[y] = jnp.broadcast_to(bias_chip, (8, CO))
    for copy in swaps:
        copy.wait_recv()

    low = lax.broadcasted_iota(jnp.int32, (144, 128), 1) < 64
    half = BLOCK // 2

    def weight_rows(part, step):
        lo_at = pl.multiple_of(part * 2 * BLOCK + core * BLOCK + step * 144, 16)
        hi_at = pl.multiple_of((part + 2) * 2 * BLOCK + core * BLOCK + step * 144, 16)
        here = slice(step * 144, step * 144 + 144)
        lo = nn(pt[pl.ds(lo_at, 144), :], dl[...]) + nn(pts[part, here, :], dls[...])
        hi = nn(pt[pl.ds(hi_at, 144), :], dlx[...]) + nn(pts[part + 2, here, :], dlsx[...])
        for n in range(4):
            cols = slice(128 * (n // 2), 128 * (n // 2) + 128)
            if n % 2:
                w[part, n, here, :] = jnp.where(low, hi[:, cols], lo[:, cols]).astype(BF16)
            else:
                w[part, n, here, :] = jnp.where(low, lo[:, cols], hi[:, cols]).astype(BF16)

    def rows_of(part):
        return pl.ds(part * half, half)

    def window(n):
        return pl.ds(pl.multiple_of(16 * (27 * lax.rem(x + n, 4) // 2), 16), WINDOW)

    def lanes_of(part):
        return pl.ds(2 * part, 2)

    turn = ((1, 0), (3, 1))
    bias_y = [remote(by.at[y], by.at[y], b_s.at[n - 1], b_r.at[n - 1], to_y(n)) for n in (1, 2, 3)]
    relay_y, relay_x, plain_y, plain_x, summed_y, summed_x = [], [], [], [], [], []

    for at, (n, part) in enumerate(turn):
        for step in range(3):
            weight_rows(0, 3 * part + step)
        relay_y.append(
            remote(
                w.at[0, lax.rem(y + 2, 4), rows_of(part), :], ya.at[at], r1_s.at[at], r1_r.at[at], to_y(n)
            )
        )
        relay_y[-1].start()
    for copy in bias_y:
        copy.start()
    for at, (n, part) in enumerate(turn):
        rows = rows_of(1 - part)
        plain_y.append(
            remote(
                w.at[0, lax.rem(y + n, 4), rows, :],
                ra.at[at, rows, :],
                r1_s.at[2 + at],
                r1_r.at[2 + at],
                to_y(n),
            )
        )
        plain_y[-1].start()
    for step in range(6):
        weight_rows(1, step)
    for at, (n, part) in enumerate(turn):
        relay_x.append(
            remote(
                w.at[1, lanes_of(part), window(2), :], xb.at[at], r1_s.at[6 + at], r1_r.at[6 + at], to_x(n)
            )
        )
        relay_x[-1].start()
    for at, (n, part) in enumerate(turn):
        lanes = lanes_of(1 - part)
        plain_x.append(
            remote(
                w.at[1, lanes, window(n), :],
                rb.at[at, lanes],
                r1_s.at[8 + at],
                r1_r.at[8 + at],
                to_x(n),
            )
        )
        plain_x[-1].start()
    for at, (n, part) in enumerate(turn):
        relay_y[at].wait_recv()
        rows = rows_of(part)
        own_part = w[0, lax.rem(y + n, 4), rows, :].astype(F32)
        ys[at] = (own_part + ya[at].astype(F32)).astype(BF16)
        summed_y.append(
            remote(ys.at[at], ra.at[at, rows, :], r1_s.at[4 + at], r1_r.at[4 + at], to_y(n))
        )
        summed_y[-1].start()
    for at, (n, part) in enumerate(turn):
        relay_x[at].wait_recv()
        own_part = w[1, lanes_of(part), window(n), :].astype(F32)
        xs[at] = (own_part + xb[at].astype(F32)).astype(BF16)
        summed_x.append(
            remote(xs.at[at], rb.at[at, lanes_of(part)], r1_s.at[10 + at], r1_r.at[10 + at], to_x(n))
        )
        summed_x[-1].start()

    for copy in bias_y:
        copy.wait_recv()
    bx[x] = by[0] + by[1] + by[2] + by[3]
    bias_x = [remote(bx.at[x], bx.at[x], b_s.at[2 + n], b_r.at[2 + n], to_x(n)) for n in (1, 2, 3)]
    for copy in bias_x:
        copy.start()

    for copy in plain_y + summed_y:
        copy.wait_recv()
    sa[...] = (w[0, y].astype(F32) + ra[0].astype(F32) + ra[1].astype(F32)).astype(BF16)
    phase2 = []
    for n in (1, 3, 2):
        start = pl.multiple_of(16 * (27 * lax.rem(x + n, 4) // 2), 16)
        phase2.append(
            remote(sa.at[pl.ds(start, WINDOW), :], ra2.at[n - 1], r2_s.at[n - 1], r2_r.at[n - 1], to_x(n))
        )
        phase2[-1].start()
    own = pl.multiple_of(16 * (27 * x // 2), 16)
    for copy in plain_x + summed_x:
        copy.wait_recv()
    sb[...] = (
        w[1, :, pl.ds(own, WINDOW), :].astype(F32) + rb[0].astype(F32) + rb[1].astype(F32)
    ).astype(BF16)
    for n in (1, 3, 2):
        phase2.append(
            remote(sb.at[lax.rem(y + n, 4)], rb2.at[n - 1], r2_s.at[2 + n], r2_r.at[2 + n], to_y(n))
        )
        phase2[-1].start()

    for copy in edges:
        copy.wait_recv()
    for f in range(3):
        for n in range(2):
            g[n, 24 + f, 8:40, :] += jnp.where(row < 7, gu[n, f], 0.0)
    sofar = take(gflat, 3 * PITCH + 39, 24, PITCH)
    put(gflat, 3 * PITCH + 39, 24, PITCH, sofar + jnp.where(col < 7, gl[...], 0.0))
    corner = jnp.where((row < 7) & (col < 7), gc[...], 0.0)
    for f in range(3):
        for n in range(2):
            g[n, 24 + f, 39:40, :] += corner[f : f + 1, 128 * n : 128 * n + 128]
    for f in range(3):
        for r in range(8):
            for n in range(2):
                vg_out[0, f, r, :, 128 * n : 128 * n + 128] = g[n, (r + 1) * 3 + f, 8:40, :].astype(BF16)


    for copy in bias_x:
        copy.wait_recv()
    bz[z] = bx[0] + bx[1] + bx[2] + bx[3]
    bias_z = [remote(bz.at[z], bz.at[z], b_s.at[5 + n], b_r.at[5 + n], to_z(n)) for n in range(1, 8)]
    for copy in bias_z:
        copy.start()

    odd = lax.rem(y, 2) == 1
    offset = 8 * lax.rem(x, 2)
    first_half = lax.broadcasted_iota(jnp.int32, (64, 128), 1) < 64
    tt[:, WINDOW:, :] = jnp.zeros((2, 24, 128), F32)
    for part in range(2):
        for copy in phase2[3 * part : 3 * part + 3]:
            copy.wait_recv()
        if part == 0:
            total = sa[pl.ds(own, WINDOW), :].astype(F32)
            for n in range(3):
                total = total + ra2[n].astype(F32)
        else:
            total = sb[y].astype(F32)
            for n in range(3):
                total = total + rb2[n].astype(F32)
        tt[part, 0:WINDOW, :] = jnp.where(odd, pltpu.roll(total, 64, 1), total)
        for half in range(2):
            u = tt[part, pl.ds(offset + PIECE * half, 128), :]
            a, b = u[0:64], u[64:128]
            zz[half * 4 + part] = jnp.where(first_half, a, pltpu.roll(b, 64, 1)).astype(BF16)
            zz[half * 4 + 2 + part] = jnp.where(first_half, pltpu.roll(a, 64, 1), b).astype(BF16)
    phase3 = []
    for n in (4, 3, 5, 2, 6, 1, 7):
        phase3.append(
            remote(zz.at[lax.rem(z + n, 8)], rz.at[n - 1], r3_s.at[n - 1], r3_r.at[n - 1], to_z(n))
        )
        phase3[-1].start()

    for copy in bias_z:
        copy.wait_recv()
    total = bz[0]
    for n in range(1, 8):
        total = total + bz[n]
    bg_out[...] = total[0:1] * FACTOR

    for copy in phase3:
        copy.wait_recv()
    total = zz[z].astype(F32)
    for n in range(7):
        total = total + rz[n].astype(F32)
    total = total * FACTOR
    turned = total.T
    kg_out[...] = jnp.concatenate([turned[0:64], turned[64:128]], axis=1)[:, 0:PIECE]

    for copies in (
        first, halos, direct, forward, relayed, swaps, passed, [swap_delta], relay_y, relay_x, plain_y, plain_x,
        summed_y, summed_x, bias_y, edges, bias_x,
        phase2, bias_z, phase3,
    ):
        for copy in copies:
            copy.wait_send()


def write_out(*refs):
    ins, outs, sem = refs[0:4], refs[4:8], refs[8]
    stores = [pltpu.make_async_copy(ins[n], outs[n], sem.at[n]) for n in range(4)]
    for copy in stores:
        copy.start()
    for copy in stores:
        copy.wait()


def body(video, kernel, bias_vec, cotangent):
    dma = pltpu.SemaphoreType.DMA
    vmem = pltpu.VMEM
    shapes = (
        jax.ShapeDtypeStruct((1, 3, 4, 16, CO), BF16),
        jax.ShapeDtypeStruct((1, 3, 8, 32, CI), BF16),
        jax.ShapeDtypeStruct((SHARD, PIECE), F32),
        jax.ShapeDtypeStruct((1, CO), F32),
    )
    operands = [
        pltpu.with_memory_space_constraint(value, pltpu.HBM)
        for value in (video, kernel.T, bias_vec.reshape(1, CO), cotangent)
    ]
    results = pl.pallas_call(
        kernel_body,
        out_shape=shapes,
        in_specs=[
            pl.BlockSpec(memory_space=pl.ANY),
            pl.BlockSpec(memory_space=pl.ANY),
            pl.BlockSpec(memory_space=pl.ANY),
            pl.BlockSpec(memory_space=pl.ANY),
        ],
        out_specs=(pl.BlockSpec(memory_space=pltpu.VMEM),) * 4,
        scratch_shapes=[
            vmem((CO, KROWS), BF16),
            vmem((3, 8, 32, CI), BF16),
            vmem((3, 4, 16, CO), BF16),
            vmem((1, CO), F32),
            vmem((2, 27, PITCH, 128), F32),
            vmem((24, CI), F32),
            vmem((8, CI), F32),
            vmem((24, CI), F32),
            vmem((3, 32, CI), BF16),
            vmem((8, CI), F32),
            vmem((TOK, KROWS), BF16),
            vmem((KROWS, TOK), BF16),
            vmem((4, BLOCK, TOK), BF16),
            vmem((TOK, CO), BF16),
            vmem((TOK, CO), BF16),
            vmem((TOK, CO), BF16),
            vmem((TOK, CO), BF16),
            vmem((2, 4, BLOCK, 128), BF16),
            vmem((2, BLOCK, 128), BF16),
            vmem((2, 4, WINDOW, 128), BF16),
            vmem((2, BLOCK // 2, 128), BF16),
            vmem((2, 2, WINDOW, 128), BF16),
            vmem((2, BLOCK // 2, 128), BF16),
            vmem((2, 2, WINDOW, 128), BF16),
            vmem((BLOCK, 128), BF16),
            vmem((4, WINDOW, 128), BF16),
            vmem((3, WINDOW, 128), BF16),
            vmem((3, WINDOW, 128), BF16),
            vmem((2, WINDOW + 24, 128), F32),
            vmem((8, 64, 128), BF16),
            vmem((7, 64, 128), BF16),
            vmem((4, 8, CO), F32),
            vmem((4, 8, CO), F32),
            vmem((8, 8, CO), F32),
            vmem((2, 27, PITCH, 128), F32),
            vmem((24, CI), F32),
            vmem((8, CI), F32),
            vmem((2, 3, 32, 128), F32),
            vmem((24, CI), F32),
            vmem((8, CI), F32),
            dma((4,)),
            dma((18,)),
            dma((18,)),
            dma((6,)),
            dma((6,)),
            dma((23,)),
            dma((23,)),
            dma((12,)),
            dma((12,)),
            dma((6,)),
            dma((6,)),
            dma((7,)),
            dma((7,)),
            dma((13,)),
            dma((13,)),
        ],
        compiler_params=pltpu.CompilerParams(
            collective_id=0, has_side_effects=True, vmem_limit_bytes=49152 * 2**10
        ),
    )(*operands)
    activated, video_grad, kernel_grad, bias_grad = pl.pallas_call(
        write_out,
        out_shape=shapes,
        in_specs=[pl.BlockSpec(memory_space=pltpu.VMEM)] * 4,
        out_specs=(pl.BlockSpec(memory_space=pl.ANY),) * 4,
        scratch_shapes=[dma((4,))],
        compiler_params=pltpu.CompilerParams(vmem_limit_bytes=4 * 2**20),
    )(*results)
    return activated, video_grad, kernel_grad.T, bias_grad.reshape(CO)


def solution(mesh):
    return jax.shard_map(
        body,
        mesh=mesh,
        in_specs=(
            P("fsdp", None, "row", "col", None),
            P(None, "fsdp"),
            P(),
            P("fsdp", None, "row", "col", None),
        ),
        out_specs=(
            P("fsdp", None, "row", "col", None),
            P("fsdp", None, "row", "col", None),
            P(("row", "col"), "fsdp"),
            P(),
        ),
        check_vma=False,
    )
```

profile of v0, /device:TPU:2, one launch (start us, length us, event | category | flops | bytes accessed | tf_op | source)
XLA Modules:
  0.0 52.5 jit_solution(5513070537120714279)
XLA Ops:
  0.6 51.1 %shard_map.75 = (bf16[1,3,4,16,256]{4,3,2,1,0:T(8,128)(2,1)S(1)}, bf16[1,3,8,32,256]{4,3,2,1,0:T(8,128)(2,1)S(1)}, f32[64,108]{1,0:T(8,128)S(1)}, f32[1,256]{1,0:T(1,128)S(1)}) custom-call(bf16[1,3,8,32,256]{4,3,2,1,0:T(8,128)(2,1)} %video.1, bf16[64,6912]{1,0:T(8,128)(2,1)} %bitcast.4, f32[1,256]{1,0:T(1,128)} %bitcast.5, bf16[1,3,4,16,256]{4,3,2,1,0:T(8,128)(2,1)} %cot.1), custom_call_target="tpu_custom_call" | custom-call | tf_op jit(solution)/shard_map/pallas_call | solution.py:591
  51.7 0.8 %shard_map.76 = (bf16[1,3,4,16,256]{4,3,2,1,0:T(8,128)(2,1)}, bf16[1,3,8,32,256]{4,3,2,1,0:T(8,128)(2,1)}, f32[64,108]{1,0:T(8,128)}, f32[1,256]{1,0:T(1,128)}) custom-call(bf16[1,3,4,16,256]{4,3,2,1,0:T(8,128)(2,1)S(1)} %get-tuple-element.12.refs_0_, bf16[1,3,8,32,256]{4,3,2,1,0:T(8,128)(2,1)S(1)} %get-tuple-element.13.refs_1_, ...), custom_call_target="tpu_custom_call" | custom-call | tf_op jit(solution)/shard_map/pallas_call | solution.py:662
where the time goes:
time: 52.8 us; the launch traced here: 52.5 us
  Pallas kernels  51.9 us (98%)
  between operations  0.64 us (1%)
    pallas_call x1, Pallas kernels, body(): pl.pallas_call(kernel_body, out_shape=shapes, in_specs=[pl.BlockSpec(memo...  51.1 us

commit v1 on v0

--- a/solution.py
+++ b/solution.py
@@ -115,6 +115,7 @@
     gu,
     gl,
     gc,
+    token,
     lsem,
     k_s,
     k_r,
@@ -165,8 +166,7 @@
         )
 
     partners = [to_y(n) for n in (1, 2, 3)] + [to_x(n) for n in (1, 2, 3)]
-    partners += [to_z(n) for n in range(1, 8)] + [sibling]
-    partners += [to_tile(a, b) for a, b in ((0, 1), (0, -1), (1, 0), (-1, 0), (1, 1), (-1, -1))]
+    partners += [to_z(1), to_z(7), sibling]
     barrier = pltpu.get_barrier_semaphore()
     for partner in partners:
         pl.semaphore_signal(barrier, inc=1, device_id=partner, device_id_type=MESH)
@@ -205,6 +205,11 @@
             )
         )
         first[-1].start()
+    def tell(step, places):
+        for place in places:
+            pl.semaphore_signal(token.at[step], inc=1, device_id=place, device_id_type=MESH)
+
+    tell(0, [to_z(1), to_z(7)])
     direct = []
     for slot, (n, part) in enumerate(((1, 0), (3, 1), (1, 1), (3, 0))):
         lanes = pl.ds(ROUND + part * SPAN, SPAN)
@@ -228,6 +233,39 @@
     hl_send[...] = take(flat, 3 * PITCH + 39, 24, PITCH)
     hc_send[0:3, :] = hl_send[21:24, :]
 
+    passed = []
+
+    def pass_on(n, start, size, slot):
+        ref = kt.at[pl.ds(shard_rows(n), 32), pl.ds(start, size)]
+        passed.append(remote(ref, ref, c_s.at[slot], c_r.at[slot], sibling))
+        passed[-1].start()
+
+    pl.semaphore_wait(token.at[0], 2)
+    tell(1, [to_z(2), to_z(6)])
+    relayed = []
+    for at, n in enumerate((1, 3, 2)):
+        if at == 2:
+            pl.semaphore_wait(token.at[1], 2)
+            tell(2, [sibling])
+        first[at].wait_recv()
+        ref = kt.at[pl.ds(shard_rows(4 - n), 32), pl.ds(via, VIA_X)]
+        for m in (1, 3, 2):
+            slot = 9 + (n - 1) * 3 + m - 1
+            relayed.append(remote(ref, ref, k_s.at[slot], k_r.at[slot], to_x(m)))
+            relayed[-1].start()
+        pass_on(4 - n, via, VIA_X, 4 + n)
+
+    pl.semaphore_wait(token.at[2], 1)
+    tell(3, [to_x(1), to_x(3)])
+    forward = []
+    for slot, (n, part) in enumerate(((1, 0), (3, 1))):
+        direct[slot].wait_recv()
+        ref = kt.at[pl.ds(shard_rows(4 - n), 32), pl.ds(ROUND + part * SPAN, SPAN)]
+        forward.append(remote(ref, ref, k_s.at[7 + slot], k_r.at[7 + slot], to_y(n)))
+        forward[-1].start()
+        pass_on(4 - n, ROUND + part * SPAN, SPAN, 17 + slot)
+
+    pl.semaphore_wait(token.at[3], 2)
     halos = [
         remote(hl_send, hl, h_s.at[0], h_r.at[0], to_tile(0, 1)),
         remote(vid.at[:, 7], hu, h_s.at[1], h_r.at[1], to_tile(1, 0)),
@@ -236,31 +274,21 @@
     for copy in halos:
         copy.start()
 
-    passed = []
-
-    def pass_on(n, start, size, slot):
-        ref = kt.at[pl.ds(shard_rows(n), 32), pl.ds(start, size)]
-        passed.append(remote(ref, ref, c_s.at[slot], c_r.at[slot], sibling))
-        passed[-1].start()
-
-    relayed = []
-    for at, n in enumerate((1, 3, 2)):
-        first[at].wait_recv()
-        ref = kt.at[pl.ds(shard_rows(4 - n), 32), pl.ds(via, VIA_X)]
-        for m in (1, 3, 2):
-            slot = 9 + (n - 1) * 3 + m - 1
-            relayed.append(remote(ref, ref, k_s.at[slot], k_r.at[slot], to_x(m)))
-            relayed[-1].start()
-        pass_on(4 - n, via, VIA_X, 4 + n)
-
-    forward = []
-    for slot, (n, part) in enumerate(((1, 0), (3, 1))):
+    def pass_relayed(at, n):
+        for k, m in enumerate((1, 3, 2)):
+            relayed[at * 3 + k].wait_recv()
+            from_x = pl.multiple_of(lax.rem(x + 4 - m, 4) * VIA_X, 128)
+            pass_on(4 - n, from_x, VIA_X, 8 + (n - 1) * 3 + m - 1)
+
+    pass_relayed(0, 1)
+    pass_relayed(1, 3)
+    for slot, (n, part) in ((2, (1, 1)), (3, (3, 0))):
         direct[slot].wait_recv()
-        ref = kt.at[pl.ds(shard_rows(4 - n), 32), pl.ds(ROUND + part * SPAN, SPAN)]
-        forward.append(remote(ref, ref, k_s.at[7 + slot], k_r.at[7 + slot], to_y(n)))
-        forward[-1].start()
         pass_on(4 - n, ROUND + part * SPAN, SPAN, 17 + slot)
-
+    pass_relayed(2, 2)
+    for part in range(2):
+        forward[part].wait_recv()
+        pass_on(2, ROUND + part * SPAN, SPAN, 21 + part)
     for copy in halos:
         copy.wait_recv()
     for f in range(3):
@@ -298,21 +326,6 @@
         swaps.append(remote(pt.at[pl.ds(base, BLOCK), :], pts.at[n], c_s.at[n], c_r.at[n], sibling))
         swaps[-1].start()
 
-    def pass_relayed(at, n):
-        for k, m in enumerate((1, 3, 2)):
-            relayed[at * 3 + k].wait_recv()
-            from_x = pl.multiple_of(lax.rem(x + 4 - m, 4) * VIA_X, 128)
-            pass_on(4 - n, from_x, VIA_X, 8 + (n - 1) * 3 + m - 1)
-
-    pass_relayed(0, 1)
-    pass_relayed(1, 3)
-    for slot, (n, part) in ((2, (1, 1)), (3, (3, 0))):
-        direct[slot].wait_recv()
-        pass_on(4 - n, ROUND + part * SPAN, SPAN, 17 + slot)
-    pass_relayed(2, 2)
-    for part in range(2):
-        forward[part].wait_recv()
-        pass_on(2, ROUND + part * SPAN, SPAN, 21 + part)
     for copy in passed:
         copy.wait_recv()
     load_k.wait()
@@ -639,6 +652,7 @@
             vmem((2, 3, 32, 128), F32),
             vmem((24, CI), F32),
             vmem((8, CI), F32),
+            pltpu.SemaphoreType.REGULAR((4,)),
             dma((4,)),
             dma((18,)),
             dma((18,)),

time: 52.8 us -> 50.8 us (0.962)
  Pallas kernels: 51.9 us -> 50 us
    pallas_call x1, Pallas kernels: 51.1 us -> 49.2 us  [body(): pl.pallas_call(kernel_body, out_shape=shapes, in_specs=[pl.BlockSpec(memo...]
where the time goes in v1:
time: 50.8 us; the launch traced here: 50.7 us
  Pallas kernels  50 us (98%)
  between operations  0.64 us (1%)
    pallas_call x1, Pallas kernels, body(): pl.pallas_call(kernel_body, out_shape=shapes, in_specs=[pl.BlockSpec(memo...  49.2 us

profile of v1, /device:TPU:2, one launch (start us, length us, event | category | flops | bytes accessed | tf_op | source)
XLA Modules:
  0.0 50.7 jit_solution(16865630181969084079)
XLA Ops:
  0.6 49.2 %shard_map.75 = (bf16[1,3,4,16,256]{4,3,2,1,0:T(8,128)(2,1)S(1)}, bf16[1,3,8,32,256]{4,3,2,1,0:T(8,128)(2,1)S(1)}, f32[64,108]{1,0:T(8,128)S(1)}, f32[1,256]{1,0:T(1,128)S(1)}) custom-call(bf16[1,3,8,32,256]{4,3,2,1,0:T(8,128)(2,1)} %video.1, bf16[64,6912]{1,0:T(8,128)(2,1)} %bitcast.4, f32[1,256]{1,0:T(1,128)} %bitcast.5, bf16[1,3,4,16,256]{4,3,2,1,0:T(8,128)(2,1)} %cot.1), custom_call_target="tpu_custom_call" | custom-call | tf_op jit(solution)/shard_map/pallas_call | solution.py:604
  49.9 0.8 %shard_map.76 = (bf16[1,3,4,16,256]{4,3,2,1,0:T(8,128)(2,1)}, bf16[1,3,8,32,256]{4,3,2,1,0:T(8,128)(2,1)}, f32[64,108]{1,0:T(8,128)}, f32[1,256]{1,0:T(1,128)}) custom-call(bf16[1,3,4,16,256]{4,3,2,1,0:T(8,128)(2,1)S(1)} %get-tuple-element.12.refs_0_, bf16[1,3,8,32,256]{4,3,2,1,0:T(8,128)(2,1)S(1)} %get-tuple-element.13.refs_1_, ...), custom_call_target="tpu_custom_call" | custom-call | tf_op jit(solution)/shard_map/pallas_call | solution.py:676
